TPU v7x, 32 devices: a whole 2x2x4 slice. The times are simulated.
32 devices in a mesh: dp: 4 (over x, core), tensor: 4 (over z), pipe: 2 (over y).
Axes of the slice: x: 2, y: 2, z: 4, core: 2. Of those that a mesh axis runs over, the one named last changes fastest.
Arguments:
- attn_policy: bfloat16 [4, 256, 4608], P('dp', 'pipe', 'tensor'), may hold values from -0.046875 to 0.046875
- attn_frozen: bfloat16 [4, 256, 4608], P('dp', 'pipe', 'tensor'), may hold values from -0.046875 to 0.046875
- readout: bfloat16 [4, 256, 8192], P('dp', 'pipe'), may hold values from -6 to 6
- rest_policy: float32 [4, 256], P('dp', 'pipe'), may hold values from -3 to 3
- rest_frozen: float32 [4, 256], P('dp', 'pipe'), may hold values from -3 to 3
- policy_out: bfloat16 [4608, 8192], P('tensor'), may hold values from -0.0625 to 0.0625
- frozen_out: bfloat16 [4608, 8192], P(('tensor', 'dp', 'pipe')), may hold values from -0.0625 to 0.0625
- rewards: float32 [4], replicated, may hold values from -4 to 4
- group_ids: int32 [4], replicated, may hold values from 0 to 1
- prompt_len: int32 [4], replicated, may hold values from 1 to 63
- response_len: int32 [4], replicated, may hold values from 64 to 192
Outputs:
- upstream_grad: bfloat16 [4, 256, 4608], P('dp', 'pipe', 'tensor')
Inputs may be any that keep to these rules, and one draw needn't show every extreme that they name: `prompt_len`: prompt and response together fit in a rollout.
All inputs are finite; a program needn't handle non-finite values.
Results may differ from a plain program's by a relative error of at most 0.001.
Values may be sent and summed in bfloat16 or wider, within the bound.
A program may use at most 128 MiB of HBM per device.

v0:
```python
import jax
import jax.numpy as jnp
from jax import lax
from jax.sharding import PartitionSpec as P

KL_WEIGHT = 0.1


def shifted(array, axis, by):
    size = lax.axis_size(axis)
    return lax.ppermute(array, axis, [(i, (i + by) % size) for i in range(size)])


def shards(
    attn_policy,
    attn_frozen,
    readout,
    rest_policy,
    rest_frozen,
    policy_out,
    frozen_out,
    rewards,
    group_ids,
    prompt_len,
    response_len,
):
    unembed = readout[0]
    local_tokens = unembed.shape[0]
    view_policy = jnp.dot(unembed, policy_out.T, preferred_element_type=jnp.float32)
    part_policy = jnp.sum(attn_policy[0].astype(jnp.float32) * view_policy, axis=1)
    frozen_rows = lax.all_gather(frozen_out, ("dp", "pipe"), axis=0, tiled=True)
    view_frozen = jnp.dot(unembed, frozen_rows.T, preferred_element_type=jnp.float32)
    part_frozen = jnp.sum(attn_frozen[0].astype(jnp.float32) * view_frozen, axis=1)
    part_policy, part_frozen = lax.psum((part_policy, part_frozen), "tensor")
    logp_policy = rest_policy[0] + part_policy
    logp_frozen = rest_frozen[0] + part_frozen
    same_group = (group_ids[:, None] == group_ids[None, :]).astype(jnp.float32)
    group_mean = jnp.dot(same_group, rewards, precision=lax.Precision.HIGHEST) / jnp.sum(
        same_group, axis=1
    )
    advantage = rewards - group_mean
    seq_index = lax.axis_index("dp")
    seq_ids = jnp.arange(rewards.shape[0], dtype=jnp.int32)
    chosen = seq_ids == seq_index
    adv_one = jnp.sum(jnp.where(chosen, advantage, 0.0))
    start_one = jnp.sum(jnp.where(chosen, prompt_len, 0))
    length_one = jnp.sum(jnp.where(chosen, response_len, 0))
    seq_total = local_tokens * lax.axis_size("pipe")
    positions = lax.axis_index("pipe") * local_tokens + jnp.arange(local_tokens, dtype=jnp.int32)
    inside = (positions >= start_one) & (positions < start_one + length_one)
    weighting = jnp.where(inside, seq_total / length_one.astype(jnp.float32), 0.0)
    log_ratio = logp_frozen - logp_policy
    slope = weighting * (KL_WEIGHT * (1.0 - jnp.exp(log_ratio)) - adv_one)
    token_grad = (slope[:, None] * view_policy).astype(jnp.bfloat16)
    received = shifted(token_grad, "pipe", -1)
    return received[None]


def solution(mesh):
    placed = (
        P("dp", "pipe", "tensor"),
        P("dp", "pipe", "tensor"),
        P("dp", "pipe", None),
        P("dp", "pipe"),
        P("dp", "pipe"),
        P("tensor", None),
        P(("tensor", "dp", "pipe"), None),
        P(),
        P(),
        P(),
        P(),
    )
    return jax.shard_map(
        shards, mesh=mesh, in_specs=placed, out_specs=P("dp", "pipe", "tensor"), check_vma=False
    )
```

profile of v0, /device:TPU:0, one launch (start us, length us, event | category | flops | bytes accessed | tf_op | source)
XLA Modules:
  0.0 151.1 jit_solution(5559983407526558518)
XLA Ops:
  6.5 0.0 copy-start
  6.5 0.0 copy-start.1
  6.5 0.0 all-gather.2.cloned.1.call-start
  6.5 0.7 all-gather.2.cloned.1.call-update
  7.3 1.3 select_reduce_fusion
  9.2 1.3 select_reduce_fusion.1
  11.8 0.9 fusion.12
  12.8 1.5 %fusion.10 = f32[]{:T(128)} fusion(f32[4]{0:T(128)} %param.18, f32[4]{0:T(128)S(1)} %fusion.12, s32[4]{0:T(128)} %param.19, s32[]{:T(128)S(6)} %axis_index.25), kind=kOutput, calls=%fused_computation.12 | convolution fusion | flops 227 | bytes 56 | tf_op jit(solution)/shard_map/dot_general | solution.py:38
  14.3 0.0 copy-done
  14.3 0.0 copy-start.2
  14.3 0.0 copy-start.3
  14.3 14.0 %fusion.9 = (f32[128]{0:T(128)S(1)}, f32[128,1152]{1,0:T(8,128)S(1)}) fusion(bf16[1,128,1152]{2,1,0:T(8,128)(2,1)} %param.11, bf16[1152,8192]{1,0:T(8,128)(2,1)} %param.16, bf16[1,128,8192]{2,1,0:T(8,128)(2,1)S(1)} %copy-done), kind=kOutput, calls=%fused_computation.10 | convolution fusion | flops 2416361472 | bytes 21856768 | tf_op jit(solution)/shard_map/dot_general | solution.py:29
  28.3 82.4 %all-gather.2.cloned.1.call-done = bf16[1152,8192]{1,0:T(8,128)(2,1)} async-done(((bf16[144,8192]{1,0:T(8,128)(2,1)}), bf16[1152,8192]{1,0:T(8,128)(2,1)}) %all-gather.2.cloned.1.call-update) | async-done | bytes 18874384 | tf_op jit(solution)/shard_map/all_gather | solution.py:31
  110.7 0.0 copy-done.1
  110.7 12.6 %fusion.3 = f32[128]{0:T(128)S(1)} fusion(bf16[1152,8192]{1,0:T(8,128)(2,1)} %all-gather.2.cloned.1.call-done, bf16[1,128,8192]{2,1,0:T(8,128)(2,1)S(1)} %copy-done, bf16[1,128,1152]{2,1,0:T(8,128)(2,1)S(1)} %copy-done.1), kind=kOutput, calls=%fused_computation.4 | convolution fusion | flops 2416361472 | bytes 21266944 | tf_op jit(solution)/shard_map/dot_general | solution.py:32
  123.3 11.7 %all-reduce = (f32[128]{0:T(128)S(1)}, f32[128]{0:T(128)S(1)}) all-reduce(f32[128]{0:T(128)S(1)} %get-tuple-element.7, f32[128]{0:T(128)S(1)} %fusion.3), channel_id=1, replica_groups=mesh['dp'=4,'tensor'=4,'pipe'=2] {'tensor'}, use_global_device_ids=true, to_apply=%region_5.6 | all-reduce | flops 256 | bytes 2048 | tf_op jit(solution)/shard_map/psum | solution.py:34
  135.0 0.0 copy-done.2
  135.0 0.0 copy-done.3
  135.0 1.3 fusion.15
  136.2 0.1 multiply_convert_fusion
  136.3 0.7 collective-permute-start
  137.1 6.5 %collective-permute-done = bf16[128,1152]{1,0:T(8,128)(2,1)S(1)} collective-permute-done((bf16[128,1152]{1,0:T(8,128)(2,1)S(1)}, bf16[128,1152]{1,0:T(8,128)(2,1)S(1)}, u32[]{:S(2)}, u32[]{:S(2)}) %collective-permute-start) | collective-permute-done | bytes 294944 | tf_op jit(solution)/shard_map/ppermute | solution.py:11
  143.6 0.7 copy.13
Async XLA Ops:
  6.5 7.8 %copy-start = (bf16[1,128,8192]{2,1,0:T(8,128)(2,1)S(1)}, bf16[1,128,8192]{2,1,0:T(8,128)(2,1)}, u32[]{:S(2)}) copy-start(bf16[1,128,8192]{2,1,0:T(8,128)(2,1)} %param.13) | copy-start | bytes 6291460
  6.5 104.2 %copy-start.1 = (bf16[1,128,1152]{2,1,0:T(8,128)(2,1)S(1)}, bf16[1,128,1152]{2,1,0:T(8,128)(2,1)}, u32[]{:S(2)}) copy-start(bf16[1,128,1152]{2,1,0:T(8,128)(2,1)} %param.12) | copy-start | bytes 884740
  6.5 104.2 %all-gather.2.cloned.1.call-start = ((), (), s32[]{:S(2)}) async-start(), calls=%async_computation | async-start | bytes 21233664 | tf_op jit(solution)/shard_map/all_gather | solution.py:31
  14.3 120.7 %copy-start.2 = (f32[1,128]{1,0:T(1,128)S(1)}, f32[1,128]{1,0:T(1,128)}, u32[]{:S(2)}) copy-start(f32[1,128]{1,0:T(1,128)} %param.14) | copy-start | bytes 1540
  14.3 120.7 %copy-start.3 = (f32[1,128]{1,0:T(1,128)S(1)}, f32[1,128]{1,0:T(1,128)}, u32[]{:S(2)}) copy-start(f32[1,128]{1,0:T(1,128)} %param.15) | copy-start | bytes 1540
  136.3 7.2 %collective-permute-start = (bf16[128,1152]{1,0:T(8,128)(2,1)S(1)}, bf16[128,1152]{1,0:T(8,128)(2,1)S(1)}, u32[]{:S(2)}, u32[]{:S(2)}) collective-permute-start(bf16[128,1152]{1,0:T(8,128)(2,1)S(1)} %multiply_convert_fusion), channel_id=1, source_target_pairs={{0,1},{1,0},{2,3},{3,2},{4,5},{5,4},{6,7},{7,6},{8,9},{9,8},{10,11... | collective-permute-start | bytes 884744 | tf_op jit(solution)/shard_map/ppermute | solution.py:11
Sparse Core Ops, SparseCore 0:
  9.2 101.4 all-gather.1
where the time goes:
time: 151 us
  waiting for transfers between devices  89.6 us (59%)
  matrix products  28.1 us (19%)
  between operations  15.4 us (10%)
  blocking collectives  11.7 us (8%)
  other arithmetic  4.9 us (3%)
    all_gather x1, waiting for transfers between devices, shards(): frozen_rows = lax.all_gather(frozen_out, ('dp', 'pipe'), axis=0, tiled=True)  82.4 us
    dot_general x1, matrix products, shards(): jnp.dot(unembed, policy_out.T, preferred_element_type=jnp.float32)  14 us
    dot_general x1, matrix products, shards(): jnp.dot(unembed, frozen_rows.T, preferred_element_type=jnp.float32)  12.6 us
    psum x1, blocking collectives, shards(): part_policy, part_frozen = lax.psum((part_policy, part_frozen), 'tensor')  11.7 us
    ppermute x1, waiting for transfers between devices, shifted(): lax.ppermute(array, axis, [(i, (i + by) % size) for i in range(size)])  6.51 us
  transfers between devices with their start and end apart: 2, of which 2 were waited for; matrix products, arithmetic and copies ran while one was open for 13% of the time, Pallas kernels for 0%

commit v1 on v0

--- a/solution.py
+++ b/solution.py
@@ -1,9 +1,270 @@
+import functools
+
 import jax
 import jax.numpy as jnp
 from jax import lax
+from jax.experimental import pallas as pl
+from jax.experimental.pallas import tpu as pltpu
 from jax.sharding import PartitionSpec as P
 
 KL_WEIGHT = 0.1
+MESH = pl.DeviceIdType.MESH
+
+SLOTS = [(e >> 2 & 1, e >> 1 & 1, e & 1) for e in range(8)]
+
+
+def related(dp, pipe, bits):
+    x, y, c = bits
+    other_x = lax.rem(dp // 2 + x, 2)
+    other_c = lax.rem(lax.rem(dp, 2) + c, 2)
+    return other_x * 2 + other_c, lax.rem(pipe + y, 2)
+
+
+def nt_dot(a, b):
+    return lax.dot_general(a, b, (((1,), (1,)), ((), ())), preferred_element_type=jnp.float32)
+
+
+def as_row(column):
+    size = column.shape[0]
+    return jnp.transpose(jnp.broadcast_to(column, (size, size)))[:1]
+
+
+def column_kernel(
+    n_t,
+    attn_p, attn_f, readout, rest_p, rest_f, policy, frozen,
+    rewards, groups, prompts, responses,
+    out,
+    abuf, rbuf, fbuf, pbuf, own, attn, view, rest, psend, precv, zsend, zrecv, grad,
+    fs, fr, as_, ar, hs, hr, rs, rr, zs, zr, ps, pr, qs, qr, gs, gr, ls, lp,
+):
+    dp, pipe, ten = lax.axis_index("dp"), lax.axis_index("pipe"), lax.axis_index("tensor")
+    n_pipe = 2
+    me = dp * n_pipe + pipe
+    core = lax.rem(dp, 2)
+    tokens = readout.shape[1]
+    rows = frozen.shape[0]
+    wide = rbuf.shape[2]
+    part = wide // n_t
+    half = tokens // 2
+    peers = [related(dp, pipe, bits) for bits in SLOTS]
+    index = [p[0] * n_pipe + p[1] for p in peers]
+    place = [{"dp": p[0], "pipe": p[1]} for p in peers]
+    column = [{"tensor": lax.rem(ten + j, n_t)} for j in range(n_t)]
+
+    def remote(source, target, send, receive, where):
+        return pltpu.make_async_remote_copy(
+            src_ref=source, dst_ref=target, send_sem=send, recv_sem=receive,
+            device_id=where, device_id_type=MESH,
+        )
+
+    def cols(start, size):
+        return pl.ds(pl.multiple_of(start, 128), size)
+
+    barrier = pltpu.get_barrier_semaphore()
+    for where in place[1:] + column[1:]:
+        pl.semaphore_signal(barrier, inc=1, device_id=where, device_id_type=MESH)
+
+    locals_ = [
+        pltpu.make_async_copy(readout.at[0], own, ls.at[0]),
+        pltpu.make_async_copy(attn_p.at[0], attn, ls.at[1]),
+        pltpu.make_async_copy(rest_p, rest.at[0], ls.at[2]),
+        pltpu.make_async_copy(rest_f, rest.at[1], ls.at[3]),
+        pltpu.make_async_copy(readout.at[0, :, cols(me * wide, wide)], rbuf.at[0], ls.at[4]),
+        pltpu.make_async_copy(attn_f.at[0], abuf.at[0], ls.at[5]),
+        pltpu.make_async_copy(
+            frozen.at[:, cols(me * wide, wide)], fbuf.at[pl.ds(pl.multiple_of(me * rows, 16), rows)], ls.at[6]
+        ),
+    ]
+    for copy in locals_:
+        copy.start()
+    chunks = policy.shape[1] // wide
+    loads = [
+        pltpu.make_async_copy(policy.at[:, pl.ds(j * wide, wide)], pbuf.at[j], lp.at[j])
+        for j in range(chunks)
+    ]
+    for copy in loads:
+        copy.start()
+
+    pl.semaphore_wait(barrier, len(place) - 1 + n_t - 1)
+
+    mine = cols(ten * part, part)
+    r_copies = {}
+    for s in (6, 7, 4, 5, 2, 3):
+        r_copies[s] = remote(
+            readout.at[0, :, cols(index[s] * wide + ten * part, part)],
+            rbuf.at[s, :, mine], rs.at[s], rr.at[s], place[s],
+        )
+    r_copies[1] = remote(
+        readout.at[0, :, cols(index[1] * wide, wide)], rbuf.at[1], rs.at[1], rr.at[1], place[1]
+    )
+    a_copies, f_copies = {}, {}
+    for s in (6, 7, 4, 5, 2, 3):
+        other_core = lax.rem(core + SLOTS[s][2], 2)
+        block = pl.ds(pl.multiple_of(other_core * half, half), half)
+        a_copies[s] = remote(
+            attn_f.at[0, block], abuf.at[s, block], as_.at[s], ar.at[s], place[s]
+        )
+    a_copies[1] = remote(attn_f.at[0], abuf.at[1], as_.at[1], ar.at[1], place[1])
+    for s in (6, 7, 4, 5, 2, 3, 1):
+        f_copies[s] = remote(
+            frozen.at[:, cols(index[s] * wide, wide)],
+            fbuf.at[pl.ds(pl.multiple_of(me * rows, 16), rows)],
+            fs.at[s], fr.at[s], place[s],
+        )
+    for s in (6, 7, 4, 5, 2, 3):
+        r_copies[s].start()
+    for s in (6, 7, 4, 5, 2, 3):
+        a_copies[s].start()
+    for s in (6, 7, 4, 5, 2, 3):
+        f_copies[s].start()
+    for s in (1,):
+        r_copies[s].start()
+        a_copies[s].start()
+        f_copies[s].start()
+
+    for s in (2, 3, 4, 5, 6, 7):
+        r_copies[s].wait_recv()
+    z_copies = [
+        remote(
+            rbuf.at[pl.ds(2, 6), :, mine], rbuf.at[pl.ds(2, 6), :, mine], zs.at[j], zr.at[j], column[j]
+        )
+        for j in range(1, n_t)
+    ]
+    for copy in z_copies:
+        copy.start()
+    block = pl.ds(pl.multiple_of(core * half, half), half)
+    h_copies = []
+    for s in (2, 3, 4, 5, 6, 7):
+        a_copies[s].wait_recv()
+        h_copies.append(
+            remote(abuf.at[s, block], abuf.at[s ^ 1, block], hs.at[s], hr.at[s ^ 1], place[1])
+        )
+        h_copies[-1].start()
+
+    for copy in locals_:
+        copy.wait()
+    view[...] = jnp.zeros_like(view)
+
+    def policy_step(j, carry):
+        pltpu.make_async_copy(policy.at[:, cols(j * wide, wide)], pbuf.at[j], lp.at[j]).wait()
+        view[...] += nt_dot(own[:, cols(j * wide, wide)], pbuf[j])
+        return carry
+
+    lax.fori_loop(0, chunks, policy_step, 0)
+    part_policy = jnp.sum(attn[...].astype(jnp.float32) * view[...], axis=1, keepdims=True)
+
+    for s in (1, 2, 3, 4, 5, 6, 7):
+        f_copies[s].wait_recv()
+    a_copies[1].wait_recv()
+    r_copies[1].wait_recv()
+    for copy in h_copies:
+        copy.wait_recv()
+    for copy in z_copies:
+        copy.wait_recv()
+
+    def frozen_step(s, carry):
+        partial = jnp.dot(abuf[s], fbuf[...], preferred_element_type=jnp.float32)
+        total = jnp.sum(partial * rbuf[s].astype(jnp.float32), axis=1, keepdims=True)
+        psend[s] = jnp.broadcast_to(as_row(total), psend.shape[1:])
+        return carry
+
+    lax.fori_loop(0, 8, frozen_step, 0)
+    p_copies = [
+        remote(psend.at[s], precv.at[s], ps.at[s], pr.at[s], place[s]) for s in range(1, 8)
+    ]
+    for copy in p_copies:
+        copy.start()
+    row_policy = jnp.broadcast_to(as_row(part_policy), psend.shape[1:])
+    total = psend[0]
+    for copy, s in zip(p_copies, range(1, 8)):
+        copy.wait_recv()
+        total += precv[s]
+    which = lax.broadcasted_iota(jnp.int32, total.shape, 0)
+    zsend[...] = jnp.where(which == 0, row_policy, total)
+    q_copies = [
+        remote(zsend, zrecv.at[j], qs.at[j], qr.at[j], column[j]) for j in range(1, n_t)
+    ]
+    for copy in q_copies:
+        copy.start()
+
+    mine_group = groups[dp]
+    sum_group, in_group = jnp.float32(0), jnp.float32(0)
+    for i in range(rewards.shape[0]):
+        same = jnp.where(groups[i] == mine_group, jnp.float32(1), jnp.float32(0))
+        sum_group += same * rewards[i]
+        in_group += same
+    def spread(value):
+        return jnp.full((1, tokens), value)
+    adv = spread(rewards[dp]) - spread(sum_group) / spread(in_group)
+    start, length = prompts[dp], responses[dp]
+    position = pipe * tokens + lax.broadcasted_iota(jnp.int32, (1, tokens), 1)
+    inside = (position >= start) & (position < start + length)
+    seq_total = tokens * n_pipe
+    weighting = jnp.where(
+        inside, jnp.float32(seq_total) / spread(length.astype(jnp.float32)), jnp.float32(0)
+    )
+
+    both = zsend[...]
+    for copy, j in zip(q_copies, range(1, n_t)):
+        copy.wait_recv()
+        both += zrecv[j]
+    log_ratio = (rest[1] + both[1:2]) - (rest[0] + both[0:1])
+    slope = weighting * (KL_WEIGHT * (1.0 - jnp.exp(log_ratio)) - adv)
+    slope = jnp.transpose(jnp.broadcast_to(slope, (tokens, tokens)))
+    for j in range(view.shape[1] // tokens):
+        at = slice(j * tokens, (j + 1) * tokens)
+        grad[:, at] = (slope * view[:, at]).astype(jnp.bfloat16)
+    last = remote(grad, out.at[0], gs, gr, place[2])
+    last.start()
+    for copies in (r_copies.values(), a_copies.values(), f_copies.values(), z_copies, h_copies, p_copies, q_copies):
+        for copy in copies:
+            copy.wait_send()
+    last.wait()
+
+
+def column_plan(n_t, *args):
+    attn_policy, readout, frozen_out = args[0], args[2], args[6]
+    tokens, width = readout.shape[1:]
+    features = attn_policy.shape[2]
+    wide = width // 8
+    any_space = pl.BlockSpec(memory_space=pl.ANY)
+    smem = pl.BlockSpec(memory_space=pltpu.SMEM)
+    bf16, f32 = jnp.bfloat16, jnp.float32
+    sems = lambda n: pltpu.SemaphoreType.DMA((n,))
+    return pl.pallas_call(
+        functools.partial(column_kernel, n_t),
+        out_shape=jax.ShapeDtypeStruct((1, tokens, features), bf16),
+        in_specs=[any_space] * 7 + [smem] * 4,
+        out_specs=any_space,
+        scratch_shapes=[
+            pltpu.VMEM((8, tokens, features), bf16),
+            pltpu.VMEM((8, tokens, wide), bf16),
+            pltpu.VMEM((features, wide), bf16),
+            pltpu.VMEM((8, features, wide), bf16),
+            pltpu.VMEM((tokens, width), bf16),
+            pltpu.VMEM((tokens, features), bf16),
+            pltpu.VMEM((tokens, features), f32),
+            pltpu.VMEM((2, 1, tokens), f32),
+            pltpu.VMEM((8, 8, tokens), f32),
+            pltpu.VMEM((8, 8, tokens), f32),
+            pltpu.VMEM((8, tokens), f32),
+            pltpu.VMEM((n_t, 8, tokens), f32),
+            pltpu.VMEM((tokens, features), bf16),
+        ]
+        + [sems(8)] * 8
+        + [sems(n_t)] * 2
+        + [sems(8)] * 2
+        + [sems(n_t)] * 2
+        + [pltpu.SemaphoreType.DMA] * 2
+        + [sems(7), sems(8)],
+        compiler_params=pltpu.CompilerParams(
+            collective_id=0, has_side_effects=True, vmem_limit_bytes=52 * 2**20
+        ),
+        cost_estimate=pl.CostEstimate(
+            flops=4 * tokens * features * width, bytes_accessed=2 * features * width + 4 * tokens * width,
+            transcendentals=tokens,
+        ),
+    )(*args)
 
 
 def shifted(array, axis, by):
@@ -11,7 +272,7 @@
     return lax.ppermute(array, axis, [(i, (i + by) % size) for i in range(size)])
 
 
-def shards(
+def gather_plan(
     attn_policy,
     attn_frozen,
     readout,
@@ -56,6 +317,14 @@
     return received[None]
 
 
+def shards(*args):
+    n_dp, n_pipe, n_t = (lax.axis_size(axis) for axis in ("dp", "pipe", "tensor"))
+    tokens, width = args[2].shape[1:]
+    if (n_dp, n_pipe) == (4, 2) and width % (8 * n_t * 128) == 0 and args[6].shape[0] % 16 == 0 and tokens == 128:
+        return column_plan(n_t, *args)
+    return gather_plan(*args)
+
+
 def solution(mesh):
     placed = (
         P("dp", "pipe", "tensor"),

time: 151 us -> 78.8 us (0.52)
  waiting for transfers between devices: 89.6 us -> 0 us
  Pallas kernels: 0 us -> 72 us
  matrix products: 28.1 us -> 0 us
  between operations: 15.4 us -> 0.02 us
  blocking collectives: 11.7 us -> 0 us
  local copies, waits for them, and re-layouts: 0.73 us -> 6.57 us
  other arithmetic: 4.9 us -> 0 us
    all_gather x1 -> x0, waiting for transfers between devices: 82.4 us -> none  [shards(): frozen_rows = lax.all_gather(frozen_out, ('dp', 'pipe'), axis=0, tiled=True)]
    pallas_call x0 -> x1, Pallas kernels: none -> 72 us  [column_plan(): pl.pallas_call(functools.partial(column_kernel, n_t), out_shape=jax.Shape...]
    dot_general x3 -> x0, matrix products: 28.1 us -> none  [the longest x1 14 us: shards(): jnp.dot(unembed, policy_out.T, preferred_element_type=jnp.float32)]
    psum x1 -> x0, blocking collectives: 11.7 us -> none  [shards(): part_policy, part_frozen = lax.psum((part_policy, part_frozen), 'tensor')]
    ppermute x1 -> x0, waiting for transfers between devices: 6.51 us -> none  [shifted(): lax.ppermute(array, axis, [(i, (i + by) % size) for i in range(size)])]
    unnamed x9 -> x17, local copies, waits for them, and re-layouts: 0.73 us -> 6.57 us
    reduce_sum x3 -> x0, other arithmetic: 3.53 us -> none  [the longest x1 1.33 us: shards(): start_one = jnp.sum(jnp.where(chosen, prompt_len, 0))]
  transfers between devices with their start and end apart: 2 -> 0, of which waited for: 2 -> 0; matrix products, arithmetic and copies ran while one was open for 13% -> 0% of each run, Pallas kernels for 0% -> 0%
where the time goes in v1:
time: 78.8 us; the launch traced here: 78.6 us
  Pallas kernels  72 us (91%)
  local copies, waits for them, and re-layouts  6.57 us (8%)
    pallas_call x1, Pallas kernels, column_plan(): pl.pallas_call(functools.partial(column_kernel, n_t), out_shape=jax.Shape...  72 us
    unnamed x17, local copies, waits for them, and re-layouts  6.57 us

profile of v1, /device:TPU:0, one launch (start us, length us, event | category | flops | bytes accessed | tf_op | source)
XLA Modules:
  0.0 78.6 jit_solution(7044151195797593771)
XLA Ops:
  0.0 0.0 copy-start
  0.0 1.0 %copy-done = bf16[1,128,1152]{2,1,0:T(8,128)(2,1)S(1)} copy-done((bf16[1,128,1152]{2,1,0:T(8,128)(2,1)S(1)}, bf16[1,128,1152]{2,1,0:T(8,128)(2,1)}, u32[]{:S(2)}) %copy-start) | copy-done | bytes 294936
  1.0 0.0 copy-start.1
  1.0 1.0 %copy-done.1 = bf16[1,128,1152]{2,1,0:T(8,128)(2,1)S(1)} copy-done((bf16[1,128,1152]{2,1,0:T(8,128)(2,1)S(1)}, bf16[1,128,1152]{2,1,0:T(8,128)(2,1)}, u32[]{:S(2)}) %copy-start.1) | copy-done | bytes 294936
  1.9 0.0 copy-start.2
  1.9 0.7 copy-done.2
  2.6 0.0 copy-start.3
  2.6 0.7 copy-done.3
  3.2 0.0 copy-start.4
  3.2 0.7 copy-done.4
  3.9 0.0 copy-start.5
  3.9 0.7 copy-done.5
  4.5 0.0 copy-start.6
  4.5 0.7 copy-done.6
  5.2 0.0 copy-start.7
  5.2 0.7 copy-done.7
  5.9 72.0 %shard_map.109 = bf16[1,128,1152]{2,1,0:T(8,128)(2,1)S(1)} custom-call(bf16[1,128,1152]{2,1,0:T(8,128)(2,1)S(1)} %copy-done, bf16[1,128,1152]{2,1,0:T(8,128)(2,1)S(1)} %copy-done.1, bf16[1,128,8192]{2,1,0:T(8,128)(2,1)} %readout.1, f32[1,128]{1,0:T(1,128)S(1)} %copy-done.2, f32[1,128]{1,0:T(1,128)S(1)} %copy-done.3, bf16[1152,8192]{1,0:T(8,128)(2,1)} %policy.1, ...), custom_call_target="tpu_custom_call" | custom-call | flops 4831838208 | bytes 23068672 | tf_op jit(solution)/shard_map/pallas_call | solution.py:234
  77.9 0.7 copy.13
Async XLA Ops:
  0.0 1.0 %copy-start = (bf16[1,128,1152]{2,1,0:T(8,128)(2,1)S(1)}, bf16[1,128,1152]{2,1,0:T(8,128)(2,1)}, u32[]{:S(2)}) copy-start(bf16[1,128,1152]{2,1,0:T(8,128)(2,1)} %attn_p.1) | copy-start | bytes 884740
  1.0 1.0 %copy-start.1 = (bf16[1,128,1152]{2,1,0:T(8,128)(2,1)S(1)}, bf16[1,128,1152]{2,1,0:T(8,128)(2,1)}, u32[]{:S(2)}) copy-start(bf16[1,128,1152]{2,1,0:T(8,128)(2,1)} %attn_f.1) | copy-start | bytes 884740
  1.9 0.7 copy-start.2
  2.6 0.7 copy-start.3
  3.2 0.7 copy-start.4
  3.9 0.7 copy-start.5
  4.5 0.7 copy-start.6
  5.2 0.7 copy-start.7

commit v2 on v1

--- a/solution.py
+++ b/solution.py
@@ -50,6 +50,7 @@
     index = [p[0] * n_pipe + p[1] for p in peers]
     place = [{"dp": p[0], "pipe": p[1]} for p in peers]
     column = [{"tensor": lax.rem(ten + j, n_t)} for j in range(n_t)]
+    everyone = {(s, j): {**place[s], **column[j]} for s in range(8) for j in range(n_t)}
 
     def remote(source, target, send, receive, where):
         return pltpu.make_async_remote_copy(
@@ -61,7 +62,7 @@
         return pl.ds(pl.multiple_of(start, 128), size)
 
     barrier = pltpu.get_barrier_semaphore()
-    for where in place[1:] + column[1:]:
+    for where in list(everyone.values())[1:]:
         pl.semaphore_signal(barrier, inc=1, device_id=where, device_id_type=MESH)
 
     locals_ = [
@@ -85,7 +86,7 @@
     for copy in loads:
         copy.start()
 
-    pl.semaphore_wait(barrier, len(place) - 1 + n_t - 1)
+    pl.semaphore_wait(barrier, 8 * n_t - 1)
 
     mine = cols(ten * part, part)
     r_copies = {}
@@ -114,32 +115,22 @@
     for s in (6, 7, 4, 5, 2, 3):
         r_copies[s].start()
     for s in (6, 7, 4, 5, 2, 3):
+        f_copies[s].start()
+    for s in (6, 7, 4, 5, 2, 3):
         a_copies[s].start()
-    for s in (6, 7, 4, 5, 2, 3):
-        f_copies[s].start()
-    for s in (1,):
-        r_copies[s].start()
-        a_copies[s].start()
-        f_copies[s].start()
-
-    for s in (2, 3, 4, 5, 6, 7):
+    r_copies[1].start()
+    a_copies[1].start()
+    f_copies[1].start()
+
+    chips = (6, 4, 2)
+    z_copies = {}
+    for s in chips:
         r_copies[s].wait_recv()
-    z_copies = [
-        remote(
-            rbuf.at[pl.ds(2, 6), :, mine], rbuf.at[pl.ds(2, 6), :, mine], zs.at[j], zr.at[j], column[j]
-        )
-        for j in range(1, n_t)
-    ]
-    for copy in z_copies:
-        copy.start()
-    block = pl.ds(pl.multiple_of(core * half, half), half)
-    h_copies = []
-    for s in (2, 3, 4, 5, 6, 7):
-        a_copies[s].wait_recv()
-        h_copies.append(
-            remote(abuf.at[s, block], abuf.at[s ^ 1, block], hs.at[s], hr.at[s ^ 1], place[1])
-        )
-        h_copies[-1].start()
+        r_copies[s + 1].wait_recv()
+        for j in range(1, n_t):
+            block = rbuf.at[pl.ds(s, 2), :, mine]
+            z_copies[s, j] = remote(block, block, zs.at[(s // 2 - 1) * n_t + j], zr.at[(s // 2 - 1) * n_t + j], column[j])
+            z_copies[s, j].start()
 
     for copy in locals_:
         copy.wait()
@@ -153,39 +144,59 @@
     lax.fori_loop(0, chunks, policy_step, 0)
     part_policy = jnp.sum(attn[...].astype(jnp.float32) * view[...], axis=1, keepdims=True)
 
-    for s in (1, 2, 3, 4, 5, 6, 7):
-        f_copies[s].wait_recv()
-    a_copies[1].wait_recv()
-    r_copies[1].wait_recv()
-    for copy in h_copies:
-        copy.wait_recv()
-    for copy in z_copies:
-        copy.wait_recv()
-
-    def frozen_step(s, carry):
-        partial = jnp.dot(abuf[s], fbuf[...], preferred_element_type=jnp.float32)
-        total = jnp.sum(partial * rbuf[s].astype(jnp.float32), axis=1, keepdims=True)
-        psend[s] = jnp.broadcast_to(as_row(total), psend.shape[1:])
-        return carry
-
-    lax.fori_loop(0, 8, frozen_step, 0)
-    p_copies = [
-        remote(psend.at[s], precv.at[s], ps.at[s], pr.at[s], place[s]) for s in range(1, 8)
-    ]
-    for copy in p_copies:
-        copy.start()
-    row_policy = jnp.broadcast_to(as_row(part_policy), psend.shape[1:])
-    total = psend[0]
-    for copy, s in zip(p_copies, range(1, 8)):
-        copy.wait_recv()
-        total += precv[s]
-    which = lax.broadcasted_iota(jnp.int32, total.shape, 0)
-    zsend[...] = jnp.where(which == 0, row_policy, total)
+    zsend[...] = as_row(part_policy)
     q_copies = [
         remote(zsend, zrecv.at[j], qs.at[j], qr.at[j], column[j]) for j in range(1, n_t)
     ]
     for copy in q_copies:
         copy.start()
+
+    p_copies = []
+
+    def frozen_step(s):
+        partial = jnp.dot(abuf[s], fbuf[...], preferred_element_type=jnp.float32)
+        total = jnp.sum(partial * rbuf[s].astype(jnp.float32), axis=1, keepdims=True)
+        psend[s] = as_row(total)
+        for j in range(n_t):
+            if s or j:
+                p_copies.append(
+                    remote(
+                        psend.at[s], precv.at[s, j], ps.at[s * n_t + j], pr.at[s * n_t + j], everyone[s, j]
+                    )
+                )
+                p_copies[-1].start()
+
+    half_block = pl.ds(pl.multiple_of(core * half, half), half)
+    h_copies = {}
+
+    def pass_on(chip):
+        for s in (chip, chip + 1):
+            a_copies[s].wait_recv()
+            h_copies[s] = remote(
+                abuf.at[s, half_block], abuf.at[s ^ 1, half_block], hs.at[s], hr.at[s ^ 1], place[1]
+            )
+            h_copies[s].start()
+
+    def remote_chip(chip):
+        for j in range(1, n_t):
+            z_copies[chip, j].wait_recv()
+        for s in (chip, chip + 1):
+            h_copies[s ^ 1].wait_recv()
+        for s in (chip, chip + 1):
+            frozen_step(s)
+
+    for s in (1, 2, 3, 4, 5, 6, 7):
+        f_copies[s].wait_recv()
+    frozen_step(0)
+    a_copies[1].wait_recv()
+    r_copies[1].wait_recv()
+    frozen_step(1)
+    pass_on(chips[0])
+    pass_on(chips[1])
+    remote_chip(chips[0])
+    pass_on(chips[2])
+    remote_chip(chips[1])
+    remote_chip(chips[2])
 
     mine_group = groups[dp]
     sum_group, in_group = jnp.float32(0), jnp.float32(0)
@@ -204,11 +215,18 @@
         inside, jnp.float32(seq_total) / spread(length.astype(jnp.float32)), jnp.float32(0)
     )
 
-    both = zsend[...]
+    policy_sum = zsend[...]
     for copy, j in zip(q_copies, range(1, n_t)):
         copy.wait_recv()
-        both += zrecv[j]
-    log_ratio = (rest[1] + both[1:2]) - (rest[0] + both[0:1])
+        policy_sum += zrecv[j]
+    for copy in p_copies:
+        copy.wait_recv()
+    frozen_sum = psend[0]
+    for s in range(8):
+        for j in range(n_t):
+            if s or j:
+                frozen_sum += precv[s, j]
+    log_ratio = (rest[1] + frozen_sum) - (rest[0] + policy_sum)
     slope = weighting * (KL_WEIGHT * (1.0 - jnp.exp(log_ratio)) - adv)
     slope = jnp.transpose(jnp.broadcast_to(slope, (tokens, tokens)))
     for j in range(view.shape[1] // tokens):
@@ -216,7 +234,7 @@
         grad[:, at] = (slope * view[:, at]).astype(jnp.bfloat16)
     last = remote(grad, out.at[0], gs, gr, place[2])
     last.start()
-    for copies in (r_copies.values(), a_copies.values(), f_copies.values(), z_copies, h_copies, p_copies, q_copies):
+    for copies in (r_copies.values(), a_copies.values(), f_copies.values(), z_copies.values(), h_copies.values(), p_copies, q_copies):
         for copy in copies:
             copy.wait_send()
     last.wait()
@@ -245,20 +263,20 @@
             pltpu.VMEM((tokens, features), bf16),
             pltpu.VMEM((tokens, features), f32),
             pltpu.VMEM((2, 1, tokens), f32),
-            pltpu.VMEM((8, 8, tokens), f32),
-            pltpu.VMEM((8, 8, tokens), f32),
-            pltpu.VMEM((8, tokens), f32),
-            pltpu.VMEM((n_t, 8, tokens), f32),
+            pltpu.VMEM((8, 1, tokens), f32),
+            pltpu.VMEM((8, n_t, 1, tokens), f32),
+            pltpu.VMEM((1, tokens), f32),
+            pltpu.VMEM((n_t, 1, tokens), f32),
             pltpu.VMEM((tokens, features), bf16),
         ]
         + [sems(8)] * 8
-        + [sems(n_t)] * 2
-        + [sems(8)] * 2
+        + [sems(3 * n_t)] * 2
+        + [sems(8 * n_t)] * 2
         + [sems(n_t)] * 2
         + [pltpu.SemaphoreType.DMA] * 2
         + [sems(7), sems(8)],
         compiler_params=pltpu.CompilerParams(
-            collective_id=0, has_side_effects=True, vmem_limit_bytes=52 * 2**20
+            collective_id=0, has_side_effects=True, vmem_limit_bytes=60 * 2**20
         ),
         cost_estimate=pl.CostEstimate(
             flops=4 * tokens * features * width, bytes_accessed=2 * features * width + 4 * tokens * width,

time: 78.8 us -> 71 us (0.901)
  local copies, waits for them, and re-layouts: 6.57 us -> 1.7 us
  Pallas kernels: 72 us -> 69.2 us
    unnamed x17 -> x1, local copies, waits for them, and re-layouts: 6.57 us -> 1.7 us
    pallas_call x1, Pallas kernels: 72 us -> 69.2 us  [column_plan(): pl.pallas_call(functools.partial(column_kernel, n_t), out_shape=jax.Shape...]
where the time goes in v2:
time: 71 us; the launch traced here: 70.9 us
  Pallas kernels  69.2 us (97%)
  local copies, waits for them, and re-layouts  1.7 us (2%)
    pallas_call x1, Pallas kernels, column_plan(): pl.pallas_call(functools.partial(column_kernel, n_t), out_shape=jax.Shape...  69.2 us
    unnamed x1, local copies, waits for them, and re-layouts  1.7 us

profile of v2, /device:TPU:0, one launch (start us, length us, event | category | flops | bytes accessed | tf_op | source)
XLA Modules:
  0.0 70.9 jit_solution(18230062724180831706)
XLA Ops:
  0.0 69.2 %shard_map.109 = bf16[1,128,1152]{2,1,0:T(8,128)(2,1)} custom-call(bf16[1,128,1152]{2,1,0:T(8,128)(2,1)} %attn_p.1, bf16[1,128,1152]{2,1,0:T(8,128)(2,1)} %attn_f.1, bf16[1,128,8192]{2,1,0:T(8,128)(2,1)} %readout.1, f32[1,128]{1,0:T(1,128)} %rest_p.1, f32[1,128]{1,0:T(1,128)} %rest_f.1, bf16[1152,8192]{1,0:T(8,128)(2,1)} %policy.1, ...), custom_call_target="tpu_custom_call" | custom-call | flops 4831838208 | bytes 23068672 | tf_op jit(solution)/shard_map/pallas_call | solution.py:252
  69.2 1.7 %copy.13 = bf16[1,128,1152]{2,1,0:T(8,128)(2,1)} copy(bf16[1,128,1152]{2,1,0:T(8,128)(2,1)} %shard_map.109) | data formatting | bytes 589824

commit v3 on v2

--- a/solution.py
+++ b/solution.py
@@ -8,6 +8,7 @@
 from jax.sharding import PartitionSpec as P
 
 KL_WEIGHT = 0.1
+EARLY = 2
 MESH = pl.DeviceIdType.MESH
 
 SLOTS = [(e >> 2 & 1, e >> 1 & 1, e & 1) for e in range(8)]
@@ -34,8 +35,8 @@
     attn_p, attn_f, readout, rest_p, rest_f, policy, frozen,
     rewards, groups, prompts, responses,
     out,
-    abuf, rbuf, fbuf, pbuf, own, attn, view, rest, psend, precv, zsend, zrecv, grad,
-    fs, fr, as_, ar, hs, hr, rs, rr, zs, zr, ps, pr, qs, qr, gs, gr, ls, lp,
+    abuf, rbuf, fbuf, pbuf, own, attn, view, rest, psend, precv, zsend, zrecv, grad, vrecv, srow, sgot,
+    fs, fr, as_, ar, hs, hr, rs, rr, zs, zr, ps, pr, qs, qr, gs, gr, ls, lp, ws, wr, vs, vr, ss, sr, os,
 ):
     dp, pipe, ten = lax.axis_index("dp"), lax.axis_index("pipe"), lax.axis_index("tensor")
     n_pipe = 2
@@ -46,6 +47,8 @@
     wide = rbuf.shape[2]
     part = wide // n_t
     half = tokens // 2
+    features = policy.shape[0]
+    cut = features - vrecv.shape[1]
     peers = [related(dp, pipe, bits) for bits in SLOTS]
     index = [p[0] * n_pipe + p[1] for p in peers]
     place = [{"dp": p[0], "pipe": p[1]} for p in peers]
@@ -99,12 +102,22 @@
         readout.at[0, :, cols(index[1] * wide, wide)], rbuf.at[1], rs.at[1], rr.at[1], place[1]
     )
     a_copies, f_copies = {}, {}
-    for s in (6, 7, 4, 5, 2, 3):
-        other_core = lax.rem(core + SLOTS[s][2], 2)
-        block = pl.ds(pl.multiple_of(other_core * half, half), half)
-        a_copies[s] = remote(
-            attn_f.at[0, block], abuf.at[s, block], as_.at[s], ar.at[s], place[s]
-        )
+
+    def half_of(which):
+        return pl.ds(pl.multiple_of(which * half, half), half)
+
+    for turn, along in enumerate((1 - core, core)):
+        for e in range(2):
+            to_core = lax.rem(core + e, 2)
+            to = {
+                "dp": lax.rem(dp // 2 + along, 2) * 2 + to_core,
+                "pipe": lax.rem(pipe + 1 - along, 2),
+            }
+            slot = 2 + 2 * along + e
+            a_copies[turn, e] = remote(
+                attn_f.at[0, half_of(to_core)], abuf.at[slot, half_of(to_core)],
+                as_.at[slot], ar.at[slot], to,
+            )
     a_copies[1] = remote(attn_f.at[0], abuf.at[1], as_.at[1], ar.at[1], place[1])
     for s in (6, 7, 4, 5, 2, 3, 1):
         f_copies[s] = remote(
@@ -114,10 +127,12 @@
         )
     for s in (6, 7, 4, 5, 2, 3):
         r_copies[s].start()
+    for e in range(2):
+        a_copies[0, e].start()
     for s in (6, 7, 4, 5, 2, 3):
         f_copies[s].start()
-    for s in (6, 7, 4, 5, 2, 3):
-        a_copies[s].start()
+    for e in range(2):
+        a_copies[1, e].start()
     r_copies[1].start()
     a_copies[1].start()
     f_copies[1].start()
@@ -131,6 +146,35 @@
             block = rbuf.at[pl.ds(s, 2), :, mine]
             z_copies[s, j] = remote(block, block, zs.at[(s // 2 - 1) * n_t + j], zr.at[(s // 2 - 1) * n_t + j], column[j])
             z_copies[s, j].start()
+
+    half_block = half_of(core)
+    h_copies, w_copies = {}, {}
+
+    def arrived(slot):
+        block = abuf.at[slot, half_block]
+        remote(block, block, as_.at[slot], ar.at[slot], place[1]).wait_recv()
+
+    def pass_on(name, slot, to_slot):
+        h_copies[name] = remote(
+            abuf.at[slot, half_block], abuf.at[to_slot, half_block], hs.at[slot], hr.at[to_slot], place[1]
+        )
+        h_copies[name].start()
+
+    def second_hop(name, slot, to_slot, where):
+        arrived(slot)
+        w_copies[name] = remote(
+            abuf.at[slot, half_block], abuf.at[to_slot, half_block], ws.at[name], wr.at[name], where
+        )
+        w_copies[name].start()
+
+    def from_core(slot):
+        block = abuf.at[slot, half_of(1 - core)]
+        remote(block, block, hs.at[slot], hr.at[slot], place[1]).wait_recv()
+
+    second_hop(0, 4 + core, 6 + core, place[2])
+    second_hop(1, 3 - core, 7 - core, place[4])
+    pass_on(0, 4 + core, 5 - core)
+    pass_on(1, 3 - core, 2 + core)
 
     for copy in locals_:
         copy.wait()
@@ -166,23 +210,11 @@
                 )
                 p_copies[-1].start()
 
-    half_block = pl.ds(pl.multiple_of(core * half, half), half)
-    h_copies = {}
-
-    def pass_on(chip):
-        for s in (chip, chip + 1):
-            a_copies[s].wait_recv()
-            h_copies[s] = remote(
-                abuf.at[s, half_block], abuf.at[s ^ 1, half_block], hs.at[s], hr.at[s ^ 1], place[1]
-            )
-            h_copies[s].start()
-
     def remote_chip(chip):
         for j in range(1, n_t):
             z_copies[chip, j].wait_recv()
         for s in (chip, chip + 1):
-            h_copies[s ^ 1].wait_recv()
-        for s in (chip, chip + 1):
+            from_core(s)
             frozen_step(s)
 
     for s in (1, 2, 3, 4, 5, 6, 7):
@@ -191,12 +223,19 @@
     a_copies[1].wait_recv()
     r_copies[1].wait_recv()
     frozen_step(1)
-    pass_on(chips[0])
-    pass_on(chips[1])
-    remote_chip(chips[0])
-    pass_on(chips[2])
-    remote_chip(chips[1])
-    remote_chip(chips[2])
+    for name in range(2):
+        w_copies[name].wait_recv()
+    pass_on(2, 6, 7)
+    pass_on(3, 7, 6)
+    remote_chip(6)
+    arrived(5 - core)
+    arrived(2 + core)
+    pass_on(4, 5 - core, 4 + core)
+    pass_on(5, 2 + core, 3 - core)
+    early = remote(view.at[:, pl.ds(cut, features - cut)], vrecv, vs, vr, place[2])
+    early.start()
+    remote_chip(4)
+    remote_chip(2)
 
     mine_group = groups[dp]
     sum_group, in_group = jnp.float32(0), jnp.float32(0)
@@ -228,16 +267,36 @@
                 frozen_sum += precv[s, j]
     log_ratio = (rest[1] + frozen_sum) - (rest[0] + policy_sum)
     slope = weighting * (KL_WEIGHT * (1.0 - jnp.exp(log_ratio)) - adv)
-    slope = jnp.transpose(jnp.broadcast_to(slope, (tokens, tokens)))
-    for j in range(view.shape[1] // tokens):
+    srow[...] = slope
+    slope_copy = remote(srow, sgot, ss, sr, place[2])
+    slope_copy.start()
+
+    def spread_rows(row):
+        return jnp.transpose(jnp.broadcast_to(row, (tokens, tokens)))
+
+    slope = spread_rows(slope)
+    for j in range(cut // tokens):
         at = slice(j * tokens, (j + 1) * tokens)
         grad[:, at] = (slope * view[:, at]).astype(jnp.bfloat16)
-    last = remote(grad, out.at[0], gs, gr, place[2])
+    first = pl.ds(0, cut)
+    last = remote(grad.at[:, first], out.at[0, :, first], gs, gr, place[2])
     last.start()
-    for copies in (r_copies.values(), a_copies.values(), f_copies.values(), z_copies.values(), h_copies.values(), p_copies, q_copies):
+    slope_copy.wait_recv()
+    early.wait_recv()
+    slope = spread_rows(sgot[...])
+    for j in range((features - cut) // tokens):
+        at = slice(j * tokens, (j + 1) * tokens)
+        grad[:, cut + j * tokens : cut + (j + 1) * tokens] = (slope * vrecv[:, at]).astype(jnp.bfloat16)
+    rest_cols = pl.ds(cut, features - cut)
+    home = pltpu.make_async_copy(grad.at[:, rest_cols], out.at[0, :, rest_cols], os)
+    home.start()
+    slope_copy.wait_send()
+    early.wait_send()
+    for copies in (r_copies.values(), a_copies.values(), f_copies.values(), z_copies.values(), h_copies.values(), w_copies.values(), p_copies, q_copies):
         for copy in copies:
             copy.wait_send()
     last.wait()
+    home.wait()
 
 
 def column_plan(n_t, *args):
@@ -268,13 +327,17 @@
             pltpu.VMEM((1, tokens), f32),
             pltpu.VMEM((n_t, 1, tokens), f32),
             pltpu.VMEM((tokens, features), bf16),
+            pltpu.VMEM((tokens, EARLY * tokens), f32),
+            pltpu.VMEM((1, tokens), f32),
+            pltpu.VMEM((1, tokens), f32),
         ]
         + [sems(8)] * 8
         + [sems(3 * n_t)] * 2
         + [sems(8 * n_t)] * 2
         + [sems(n_t)] * 2
         + [pltpu.SemaphoreType.DMA] * 2
-        + [sems(7), sems(8)],
+        + [sems(7), sems(8), sems(2), sems(2)]
+        + [pltpu.SemaphoreType.DMA] * 5,
         compiler_params=pltpu.CompilerParams(
             collective_id=0, has_side_effects=True, vmem_limit_bytes=60 * 2**20
         ),

time: 71 us -> 68.6 us (0.966)
  Pallas kernels: 69.2 us -> 66.8 us
    pallas_call x1, Pallas kernels: 69.2 us -> 66.8 us  [column_plan(): pl.pallas_call(functools.partial(column_kernel, n_t), out_shape=jax.Shape...]
where the time goes in v3:
time: 68.6 us; the launch traced here: 68.5 us
  Pallas kernels  66.8 us (97%)
  local copies, waits for them, and re-layouts  1.7 us (2%)
    pallas_call x1, Pallas kernels, column_plan(): pl.pallas_call(functools.partial(column_kernel, n_t), out_shape=jax.Shape...  66.8 us
    unnamed x1, local copies, waits for them, and re-layouts  1.7 us

profile of v3, /device:TPU:0, one launch (start us, length us, event | category | flops | bytes accessed | tf_op | source)
XLA Modules:
  0.0 68.5 jit_solution(8863396182543608782)
XLA Ops:
  0.0 66.8 %shard_map.109 = bf16[1,128,1152]{2,1,0:T(8,128)(2,1)} custom-call(bf16[1,128,1152]{2,1,0:T(8,128)(2,1)} %attn_p.1, bf16[1,128,1152]{2,1,0:T(8,128)(2,1)} %attn_f.1, bf16[1,128,8192]{2,1,0:T(8,128)(2,1)} %readout.1, f32[1,128]{1,0:T(1,128)} %rest_p.1, f32[1,128]{1,0:T(1,128)} %rest_f.1, bf16[1152,8192]{1,0:T(8,128)(2,1)} %policy.1, ...), custom_call_target="tpu_custom_call" | custom-call | flops 4831838208 | bytes 23068672 | tf_op jit(solution)/shard_map/pallas_call | solution.py:311
  66.8 1.7 %copy.13 = bf16[1,128,1152]{2,1,0:T(8,128)(2,1)} copy(bf16[1,128,1152]{2,1,0:T(8,128)(2,1)} %shard_map.109) | data formatting | bytes 589824
